TPU v7x, 32 devices: a whole 2x2x4 slice. The times are simulated.
32 devices in a mesh: blk: 8 (over y, x, core), grp: 4 (over z).
Axes of the slice: x: 2, y: 2, z: 4, core: 2. Of those that a mesh axis runs over, the one named last changes fastest.
Arguments:
- picture_embedding: bfloat16 [12288, 1152], P(('blk', 'grp')), may hold values from -1.5 to 1.5
- caption_embedding: bfloat16 [12288, 1152], P(('blk', 'grp')), may hold values from -1.5 to 1.5
- inverse_warmth: float32 [], replicated, may hold values from 2 to 10
- additive_offset: float32 [], replicated, may hold values from -4 to 0
- matching_caption_group: int32 [12288], P(('blk', 'grp')), may hold values from 0 to 2
- matching_caption_entry: int32 [12288], P(('blk', 'grp')), may hold values from 0 to 383
Outputs:
- grad_image: bfloat16 [12288, 1152], P(('blk', 'grp'))
- grad_text: bfloat16 [12288, 1152], P(('blk', 'grp'))
Inputs may be any that keep to these rules, and one draw needn't show every extreme that they name: matching_caption_group[i] names the window block k - 1 + matching_caption_group[i] of image i's block k.
All inputs are finite; a program needn't handle non-finite values.
Results may differ from a plain program's by a relative error of at most 0.007.
Values may be sent and summed in bfloat16 or wider, within the bound.
A program may use at most 64 MiB of HBM per device.

v0:
```python
import jax
import jax.numpy as jnp
from jax import lax
from jax.sharding import PartitionSpec as P


def extended(shard, sides, width):
    for axis, dim in sides:
        size, length = (lax.axis_size(axis), shard.shape[dim])
        up = [(i, (i + 1) % size) for i in range(size)]
        down = [(j, i) for i, j in up]
        last = lax.slice_in_dim(shard, length - width, length, axis=dim)
        initial = lax.slice_in_dim(shard, 0, width, axis=dim)
        before = lax.ppermute(last, axis, up)
        after = lax.ppermute(initial, axis, down)
        shard = jnp.concatenate([before, shard, after], axis=dim)
    return shard


def from_behind(shard, axis, by):
    length = lax.axis_size(axis)
    return lax.ppermute(shard, axis, [(i, (i + by) % length) for i in range(length)])


def logistic_slices(picture_entries, adjacent_reach, target_signs, inverse_warmth, additive_offset):
    similarity_values = jnp.einsum(
        "rd,cd->rc", picture_entries, adjacent_reach, preferred_element_type=jnp.float32
    )
    similarity_raw = inverse_warmth * similarity_values + additive_offset
    column_index = lax.broadcasted_iota(jnp.int32, similarity_raw.shape, 1)
    pair_sign = jnp.where(
        column_index == target_signs[:, None], jnp.float32(1.0), jnp.float32(-1.0)
    )
    return (-pair_sign * jax.nn.sigmoid(-pair_sign * similarity_raw)).astype(jnp.bfloat16)


def per_device(
    picture_embedding,
    caption_embedding,
    inverse_warmth,
    additive_offset,
    matching_caption_group,
    matching_caption_entry,
):
    row_count = picture_embedding.shape[0]
    target_signs = matching_caption_group * row_count + matching_caption_entry
    adjacent_reach = extended(caption_embedding, ((("blk", "grp"), 0),), row_count)
    derivative_slices = logistic_slices(
        picture_embedding, adjacent_reach, target_signs, inverse_warmth, additive_offset
    )
    grad_image = (
        inverse_warmth
        * jnp.dot(derivative_slices, adjacent_reach, preferred_element_type=jnp.float32)
    ).astype(jnp.bfloat16)
    incomplete_portion = inverse_warmth * jnp.einsum(
        "rc,rd->cd", derivative_slices, picture_embedding, preferred_element_type=jnp.float32
    )
    from_after = from_behind(
        incomplete_portion[:row_count].astype(jnp.bfloat16), ("blk", "grp"), -1
    ).astype(jnp.float32)
    from_before = from_behind(
        incomplete_portion[2 * row_count :].astype(jnp.bfloat16), ("blk", "grp"), 1
    ).astype(jnp.float32)
    grad_text = (incomplete_portion[row_count : 2 * row_count] + from_after + from_before).astype(
        jnp.bfloat16
    )
    return (grad_image, grad_text)


def solution(mesh):
    placed = (
        P(("blk", "grp"), None),
        P(("blk", "grp"), None),
        P(),
        P(),
        P(("blk", "grp")),
        P(("blk", "grp")),
    )
    return jax.shard_map(
        per_device,
        mesh=mesh,
        in_specs=placed,
        out_specs=(P(("blk", "grp"), None), P(("blk", "grp"), None)),
        check_vma=False,
    )
```

profile of v0, /device:TPU:1, one launch (start us, length us, event | category | flops | bytes accessed | tf_op | source)
XLA Modules:
  0.0 90.5 jit_solution(681934495282285691)
XLA Ops:
  0.6 0.0 copy-start
  0.6 0.0 copy-start.1
  0.7 2.2 %collective-permute-start = (bf16[384,1152]{1,0:T(8,128)(2,1)}, bf16[384,1152]{1,0:T(8,128)(2,1)S(1)}, u32[]{:S(2)}, u32[]{:S(2)}) collective-permute-start(bf16[384,1152]{1,0:T(8,128)(2,1)} %param.7), channel_id=1, source_target_pairs={{0,1},{1,2},{2,3},{3,4},{4,5},{5,6},{6,7},{7,8},{8,9},{9,10},{10,1... | collective-permute-start | bytes 2654216 | tf_op jit(solution)/shard_map/ppermute | solution.py:14
  2.8 2.7 %collective-permute-start.1 = (bf16[384,1152]{1,0:T(8,128)(2,1)}, bf16[384,1152]{1,0:T(8,128)(2,1)S(1)}, u32[]{:S(2)}, u32[]{:S(2)}) collective-permute-start(bf16[384,1152]{1,0:T(8,128)(2,1)} %param.7), channel_id=1, source_target_pairs={{1,0},{2,1},{3,2},{4,3},{5,4},{6,5},{7,6},{8,7},{9,8},{10,9},{11,1... | collective-permute-start | bytes 2654216 | tf_op jit(solution)/shard_map/ppermute | solution.py:15
  6.8 0.7 multiply_add_fusion
  7.5 18.2 %collective-permute-done = bf16[384,1152]{1,0:T(8,128)(2,1)S(1)} collective-permute-done((bf16[384,1152]{1,0:T(8,128)(2,1)}, bf16[384,1152]{1,0:T(8,128)(2,1)S(1)}, u32[]{:S(2)}, u32[]{:S(2)}) %collective-permute-start) | collective-permute-done | bytes 884768 | tf_op jit(solution)/shard_map/ppermute | solution.py:14
  25.7 0.1 constant_dynamic-update-slice_fusion.2
  25.7 0.0 copy-done.1
  25.8 0.1 constant_dynamic-update-slice_fusion.1
  25.9 16.3 %collective-permute-done.1 = bf16[384,1152]{1,0:T(8,128)(2,1)S(1)} collective-permute-done((bf16[384,1152]{1,0:T(8,128)(2,1)}, bf16[384,1152]{1,0:T(8,128)(2,1)S(1)}, u32[]{:S(2)}, u32[]{:S(2)}) %collective-permute-start.1) | collective-permute-done | bytes 884768 | tf_op jit(solution)/shard_map/ppermute | solution.py:15
  42.2 0.1 constant_dynamic-update-slice_fusion
  42.3 0.0 copy-done
  42.3 2.2 %fusion.8 = bf16[384,1152]{0,1:T(8,128)(2,1)S(1)} fusion(bf16[1152,1152]{1,0:T(8,128)(2,1)S(1)} %constant_dynamic-update-slice_fusion, bf16[384,1152]{1,0:T(8,128)(2,1)S(1)} %copy-done, f32[]{:T(128)S(6)} %copy.11, f32[]{:T(128)S(6)} %copy.10, s32[384]{0:T(512)S(1)} %multiply_add_fusion), kind=kOutput, calls=%fused_computation.11 | convolution fusion | flops 1024081920 | bytes 4425224 | tf_op jit(solution)/shard_map/rd,cd->rc/dot_general | solution.py:26
  44.5 1.6 %fusion.13 = (bf16[1152,1152]{1,0:T(8,128)(2,1)S(1)}, f32[1152,1152]{1,0:T(8,128)S(1)}) fusion(bf16[384,1152]{0,1:T(8,128)(2,1)S(1)} %fusion.8, bf16[384,1152]{1,0:T(8,128)(2,1)S(1)} %copy-done, f32[]{:T(128)S(6)} %copy.10), kind=kOutput, calls=%fused_computation.22 | convolution fusion | flops 1021870080 | bytes 9732100 | tf_op jit(solution)/shard_map/rc,rd->cd/dot_general | solution.py:55
  46.1 0.1 fusion.12
  46.3 4.1 %collective-permute-start.2 = (bf16[384,1152]{1,0:T(8,128)(2,1)S(1)}, bf16[384,1152]{1,0:T(8,128)(2,1)S(1)}, u32[]{:S(2)}, u32[]{:S(2)}) collective-permute-start(bf16[384,1152]{1,0:T(8,128)(2,1)S(1)} %get-tuple-element.2), channel_id=1, source_target_pairs={{0,31},{1,0},{2,1},{3,2},{4,3},{5,4},{6,5},{7,6},{8,7},{9,8},{10,9... | collective-permute-start | bytes 2654216 | tf_op jit(solution)/shard_map/ppermute | solution.py:22
  50.3 0.0 collective-permute-start.3
  50.3 2.4 %fusion.9 = bf16[384,1152]{1,0:T(8,128)(2,1)} fusion(bf16[384,1152]{0,1:T(8,128)(2,1)S(1)} %fusion.8, bf16[1152,1152]{1,0:T(8,128)(2,1)S(1)} %constant_dynamic-update-slice_fusion, f32[]{:T(128)S(6)} %copy.10), kind=kOutput, calls=%fused_computation.12 | convolution fusion | flops 1020100608 | bytes 4423684 | tf_op jit(solution)/shard_map/dot_general | solution.py:53
  52.7 15.6 %collective-permute-done.2 = bf16[384,1152]{1,0:T(8,128)(2,1)S(1)} collective-permute-done((bf16[384,1152]{1,0:T(8,128)(2,1)S(1)}, bf16[384,1152]{1,0:T(8,128)(2,1)S(1)}, u32[]{:S(2)}, u32[]{:S(2)}) %collective-permute-start.2) | collective-permute-done | bytes 884768 | tf_op jit(solution)/shard_map/ppermute | solution.py:22
  68.3 21.0 %collective-permute-done.3 = bf16[384,1152]{1,0:T(8,128)(2,1)S(1)} collective-permute-done((bf16[384,1152]{1,0:T(8,128)(2,1)S(1)}, bf16[384,1152]{1,0:T(8,128)(2,1)S(1)}, u32[]{:S(2)}, u32[]{:S(2)}) %collective-permute-start.3) | collective-permute-done | bytes 884768 | tf_op jit(solution)/shard_map/ppermute | solution.py:22
  89.3 1.2 %fusion.11 = bf16[384,1152]{1,0:T(8,128)(2,1)} fusion(f32[1152,1152]{1,0:T(8,128)S(1)} %get-tuple-element.5, bf16[384,1152]{1,0:T(8,128)(2,1)S(1)} %collective-permute-done.3, bf16[384,1152]{1,0:T(8,128)(2,1)S(1)} %collective-permute-done.2), kind=kLoop, calls=%fused_computation.15 | loop fusion | flops 2211840 | bytes 4423680 | tf_op jit(solution)/shard_map/convert_element_type | solution.py:64
Async XLA Ops:
  0.6 41.7 %copy-start = (bf16[384,1152]{1,0:T(8,128)(2,1)S(1)}, bf16[384,1152]{1,0:T(8,128)(2,1)}, u32[]{:S(2)}) copy-start(bf16[384,1152]{1,0:T(8,128)(2,1)} %param.6) | copy-start | bytes 2654212
  0.6 25.1 %copy-start.1 = (bf16[384,1152]{1,0:T(8,128)(2,1)S(1)}, bf16[384,1152]{1,0:T(8,128)(2,1)}, u32[]{:S(2)}) copy-start(bf16[384,1152]{1,0:T(8,128)(2,1)} %param.7) | copy-start | bytes 2654212
  0.7 25.0 %collective-permute-start = (bf16[384,1152]{1,0:T(8,128)(2,1)}, bf16[384,1152]{1,0:T(8,128)(2,1)S(1)}, u32[]{:S(2)}, u32[]{:S(2)}) collective-permute-start(bf16[384,1152]{1,0:T(8,128)(2,1)} %param.7), channel_id=1, source_target_pairs={{0,1},{1,2},{2,3},{3,4},{4,5},{5,6},{6,7},{7,8},{8,9},{9,10},{10,1... | collective-permute-start | bytes 2654216 | tf_op jit(solution)/shard_map/ppermute | solution.py:14
  2.8 39.4 %collective-permute-start.1 = (bf16[384,1152]{1,0:T(8,128)(2,1)}, bf16[384,1152]{1,0:T(8,128)(2,1)S(1)}, u32[]{:S(2)}, u32[]{:S(2)}) collective-permute-start(bf16[384,1152]{1,0:T(8,128)(2,1)} %param.7), channel_id=1, source_target_pairs={{1,0},{2,1},{3,2},{4,3},{5,4},{6,5},{7,6},{8,7},{9,8},{10,9},{11,1... | collective-permute-start | bytes 2654216 | tf_op jit(solution)/shard_map/ppermute | solution.py:15
  46.3 22.1 %collective-permute-start.2 = (bf16[384,1152]{1,0:T(8,128)(2,1)S(1)}, bf16[384,1152]{1,0:T(8,128)(2,1)S(1)}, u32[]{:S(2)}, u32[]{:S(2)}) collective-permute-start(bf16[384,1152]{1,0:T(8,128)(2,1)S(1)} %get-tuple-element.2), channel_id=1, source_target_pairs={{0,31},{1,0},{2,1},{3,2},{4,3},{5,4},{6,5},{7,6},{8,7},{9,8},{10,9... | collective-permute-start | bytes 2654216 | tf_op jit(solution)/shard_map/ppermute | solution.py:22
  50.3 39.0 %collective-permute-start.3 = (bf16[384,1152]{1,0:T(8,128)(2,1)S(1)}, bf16[384,1152]{1,0:T(8,128)(2,1)S(1)}, u32[]{:S(2)}, u32[]{:S(2)}) collective-permute-start(bf16[384,1152]{1,0:T(8,128)(2,1)S(1)} %get-tuple-element.3), channel_id=1, source_target_pairs={{0,1},{1,2},{2,3},{3,4},{4,5},{5,6},{6,7},{7,8},{8,9},{9,10},{10,1... | collective-permute-start | bytes 2654216 | tf_op jit(solution)/shard_map/ppermute | solution.py:22
where the time goes:
time: 90.7 us; the launch traced here: 90.5 us
  waiting for transfers between devices  71.1 us (78%)
  starting transfers between devices  8.9 us (10%)
  matrix products  6.12 us (7%)
  between operations  2 us (2%)
  other arithmetic  1.88 us (2%)
    ppermute x2, waiting for transfers between devices, from_behind(): lax.ppermute(shard, axis, [(i, (i + by) % length) for i in range(length)])  36.6 us
    ppermute x1, waiting for transfers between devices, extended(): before = lax.ppermute(last, axis, up)  18.2 us
    ppermute x1, waiting for transfers between devices, extended(): after = lax.ppermute(initial, axis, down)  16.3 us
    ppermute x2, starting transfers between devices, from_behind(): lax.ppermute(shard, axis, [(i, (i + by) % length) for i in range(length)])  4.06 us
    ppermute x1, starting transfers between devices, extended(): after = lax.ppermute(initial, axis, down)  2.65 us
    dot_general x1, matrix products, per_device(): jnp.dot(derivative_slices, adjacent_reach, preferred_element_type=jnp.flo...  2.36 us
    ppermute x1, starting transfers between devices, extended(): before = lax.ppermute(last, axis, up)  2.18 us
    dot_general x1, matrix products, logistic_slices(): jnp.einsum('rd,cd->rc', picture_entries, adjacent_reach, preferred_elemen...  2.15 us
  transfers between devices with their start and end apart: 4, of which 4 were waited for; matrix products, arithmetic and copies ran while one was open for 4% of the time, Pallas kernels for 0%

commit v1 on v0

v1 whole, which is shorter than its diff:
```python
import functools

import jax
import jax.numpy as jnp
from jax import lax
from jax.experimental import pallas as pl
from jax.experimental.pallas import tpu as pltpu
from jax.sharding import PartitionSpec as P

MESH = pl.DeviceIdType.MESH
LANES = 128
WINDOW = 2


def kernel(
    axes,
    sizes,
    pieces,
    group_ref,
    entry_ref,
    warmth_ref,
    offset_ref,
    picture_hbm,
    caption_hbm,
    grad_image_ref,
    grad_text_ref,
    picture,
    caption,
    target,
    far_picture,
    far_caption,
    far_target,
    image_sum,
    text_sum,
    local_sem,
    send_sem,
    recv_sem,
):
    rows = picture.shape[0]
    outer, inner = sizes
    count = outer * inner
    me = lax.axis_index(axes[0]) * inner + lax.axis_index(axes[1])

    def place(index):
        return {axes[0]: index // inner, axes[1]: lax.rem(index, inner)}

    right = place(lax.rem(me + 1, count))
    left = place(lax.rem(me + count - 1, count))

    barrier = pltpu.get_barrier_semaphore()
    for neighbour in (left, right):
        pl.semaphore_signal(barrier, inc=1, device_id=neighbour, device_id_type=MESH)
    load_picture = pltpu.make_async_copy(picture_hbm, picture, local_sem.at[0])
    load_caption = pltpu.make_async_copy(caption_hbm, caption, local_sem.at[1])
    load_picture.start()
    load_caption.start()
    target[...] = jnp.broadcast_to(
        group_ref[...] * rows + entry_ref[...], target.shape
    )
    pl.semaphore_wait(barrier, 2)

    def send(piece, slot):
        kind, start, size = pieces[piece]
        if kind == "target":
            source, sink = target, far_target.at[slot]
        elif kind == "caption":
            source = caption_hbm.at[pl.ds(start, size)]
            sink = far_caption.at[slot, pl.ds(start, size)]
        else:
            source = picture_hbm.at[pl.ds(start, size)]
            sink = far_picture.at[slot, pl.ds(start, size)]
        return pltpu.make_async_remote_copy(
            src_ref=source,
            dst_ref=sink,
            send_sem=send_sem.at[slot, piece],
            recv_sem=recv_sem.at[slot, piece],
            device_id=(right, left)[slot],
            device_id_type=MESH,
        )

    sends = [[send(piece, slot) for slot in (0, 1)] for piece in range(len(pieces))]
    started = 0
    for piece in range(min(1 + WINDOW, len(pieces))):
        for copy in sends[piece]:
            copy.start()
        started += 1
    sent = 0

    warmth = warmth_ref[0]
    offset = offset_ref[0]

    def tile(text, image, image_target, first):
        logit = warmth * lax.dot_general(
            text, image, (((1,), (1,)), ((), ())), preferred_element_type=jnp.float32
        ) + offset
        row = lax.broadcasted_iota(jnp.int32, logit.shape, 0) + first
        match = row == image_target
        value = jax.nn.sigmoid(jnp.where(match, -logit, logit))
        return jnp.where(match, -value, value).astype(jnp.bfloat16)

    def over_text(values, text):
        return lax.dot_general(
            values, text, (((0,), (0,)), ((), ())), preferred_element_type=jnp.float32
        )

    load_picture.wait()
    load_caption.wait()
    own = tile(caption[...], picture[...], target[0:1, :], rows)
    text_sum[...] = jnp.dot(own, picture[...], preferred_element_type=jnp.float32)
    image_sum[...] = over_text(own, caption[...])

    captions_left = sum(kind == "caption" for kind, _, _ in pieces)
    for piece, (kind, start, size) in enumerate(pieces):
        if piece >= 1 and started < len(pieces):
            for copy in sends[piece]:
                copy.wait_send()
            sent = piece + 1
            for copy in sends[started]:
                copy.start()
            started += 1
        for slot in (0, 1):
            sends[piece][slot].wait_recv()
            if kind == "caption":
                text = far_caption[slot, pl.ds(start, size)]
                values = tile(text, picture[...], target[0:1, :], 2 * slot * rows + start)
                image_sum[...] += over_text(values, text)
            elif kind == "picture":
                image = far_picture[slot, pl.ds(start, size)]
                values = tile(
                    caption[...],
                    image,
                    far_target[slot, 0:1, pl.ds(start, size)],
                    2 * (1 - slot) * rows,
                )
                text_sum[...] += jnp.dot(
                    values, image, preferred_element_type=jnp.float32
                )
        if kind == "caption":
            captions_left -= 1
            if captions_left == 0:
                grad_image_ref[...] = (warmth * image_sum[...]).astype(
                    grad_image_ref.dtype
                )
    grad_text_ref[...] = (warmth * text_sum[...]).astype(grad_text_ref.dtype)
    for piece in range(len(pieces)):
        if piece == 0 or piece >= sent:
            for copy in sends[piece]:
                copy.wait_send()


def per_device(
    axes,
    sizes,
    picture_embedding,
    caption_embedding,
    inverse_warmth,
    additive_offset,
    matching_caption_group,
    matching_caption_entry,
):
    rows, width = picture_embedding.shape
    chunk = LANES if rows % LANES == 0 else rows
    pieces = [("target", 0, rows), ("caption", 0, rows)]
    pieces += [("picture", start, chunk) for start in range(0, rows, chunk)]
    block = (rows, width)
    vmem = pl.BlockSpec(memory_space=pltpu.VMEM)
    smem = pl.BlockSpec(memory_space=pltpu.SMEM)
    hbm = pl.BlockSpec(memory_space=pl.ANY)
    out = jax.ShapeDtypeStruct(block, jnp.bfloat16)
    return pl.pallas_call(
        functools.partial(kernel, axes, sizes, pieces),
        out_shape=(out, out),
        in_specs=[vmem, vmem, smem, smem, hbm, hbm],
        out_specs=(vmem, vmem),
        scratch_shapes=[
            pltpu.VMEM(block, jnp.bfloat16),
            pltpu.VMEM(block, jnp.bfloat16),
            pltpu.VMEM((8, rows), jnp.int32),
            pltpu.VMEM((2,) + block, jnp.bfloat16),
            pltpu.VMEM((2,) + block, jnp.bfloat16),
            pltpu.VMEM((2, 8, rows), jnp.int32),
            pltpu.VMEM(block, jnp.float32),
            pltpu.VMEM(block, jnp.float32),
            pltpu.SemaphoreType.DMA((2,)),
            pltpu.SemaphoreType.DMA((2, len(pieces))),
            pltpu.SemaphoreType.DMA((2, len(pieces))),
        ],
        compiler_params=pltpu.CompilerParams(
            collective_id=0, has_side_effects=True, vmem_limit_bytes=32 << 20
        ),
    )(
        matching_caption_group.reshape(1, rows),
        matching_caption_entry.reshape(1, rows),
        inverse_warmth.reshape(1),
        additive_offset.reshape(1),
        picture_embedding,
        caption_embedding,
    )


def solution(mesh):
    axes = ("blk", "grp")
    sizes = tuple(mesh.shape[axis] for axis in axes)
    placed = (
        P(axes, None),
        P(axes, None),
        P(),
        P(),
        P(axes),
        P(axes),
    )
    return jax.shard_map(
        functools.partial(per_device, axes, sizes),
        mesh=mesh,
        in_specs=placed,
        out_specs=(P(axes, None), P(axes, None)),
        check_vma=False,
    )
```

time: 90.7 us -> 90.3 us (level)
  the two profiles are of different devices: /device:TPU:1 before, /device:TPU:27 now
where the time goes in v1:
time: 90.3 us; the launch traced here: 90.1 us
  Pallas kernels  83.3 us (92%)
  local copies, waits for them, and re-layouts  4.85 us (5%)
  between operations  1.97 us (2%)
    pallas_call x1, Pallas kernels, per_device(): pl.pallas_call(functools.partial(kernel, axes, sizes, pieces), out_shape=...  83.3 us
    unnamed x10, local copies, waits for them, and re-layouts  4.84 us

profile of v1, /device:TPU:27, one launch (start us, length us, event | category | flops | bytes accessed | tf_op | source)
XLA Modules:
  0.0 90.1 jit_solution(16167701101673313559)
XLA Ops:
  1.3 0.0 copy-start.2
  1.9 0.0 copy-done.2
  2.0 0.0 copy-start.3
  2.0 0.7 copy-done.3
  2.6 0.0 copy-start
  2.6 1.2 %copy-done = bf16[384,1152]{1,0:T(8,128)(2,1)S(1)} copy-done((bf16[384,1152]{1,0:T(8,128)(2,1)S(1)}, bf16[384,1152]{1,0:T(8,128)(2,1)}, u32[]{:S(2)}) %copy-start) | copy-done | bytes 884760
  3.8 0.0 copy-start.1
  3.8 1.2 %copy-done.1 = bf16[384,1152]{1,0:T(8,128)(2,1)S(1)} copy-done((bf16[384,1152]{1,0:T(8,128)(2,1)S(1)}, bf16[384,1152]{1,0:T(8,128)(2,1)}, u32[]{:S(2)}) %copy-start.1) | copy-done | bytes 884760
  5.0 83.3 %shard_map.77 = (bf16[384,1152]{1,0:T(8,128)(2,1)S(1)}, bf16[384,1152]{1,0:T(8,128)(2,1)S(1)}) custom-call(s32[1,384]{1,0:T(1,128)S(1)} %reshape.16.group_ref, s32[1,384]{1,0:T(1,128)S(1)} %reshape.17.entry_ref, f32[1]{0:T(128)} %bitcast.2.warmth_ref, f32[1]{0:T(128)} %bitcast.3.offset_ref, bf16[384,1152]{1,0:T(8,128)(2,1)S(1)} %copy-done, ...), custom_call_target="tpu_custom_call" | custom-call | tf_op jit(solution)/shard_map/pallas_call | solution.py:170
  88.3 0.9 %copy.12 = bf16[384,1152]{1,0:T(8,128)(2,1)} copy(bf16[384,1152]{1,0:T(8,128)(2,1)S(1)} %get-tuple-element.4) | data formatting | bytes 1769472
  89.2 0.9 %copy.13 = bf16[384,1152]{1,0:T(8,128)(2,1)} copy(bf16[384,1152]{1,0:T(8,128)(2,1)S(1)} %get-tuple-element.5) | data formatting | bytes 1769472
  (2 shorter events, 0.0 us)
Async XLA Ops:
  1.3 0.7 copy-start.2
  2.0 0.7 copy-start.3
  2.6 1.2 %copy-start = (bf16[384,1152]{1,0:T(8,128)(2,1)S(1)}, bf16[384,1152]{1,0:T(8,128)(2,1)}, u32[]{:S(2)}) copy-start(bf16[384,1152]{1,0:T(8,128)(2,1)} %picture_hbm.1) | copy-start | bytes 2654212
  3.8 1.2 %copy-start.1 = (bf16[384,1152]{1,0:T(8,128)(2,1)S(1)}, bf16[384,1152]{1,0:T(8,128)(2,1)}, u32[]{:S(2)}) copy-start(bf16[384,1152]{1,0:T(8,128)(2,1)} %caption_hbm.1) | copy-start | bytes 2654212

commit v2 on v1

--- a/solution.py
+++ b/solution.py
@@ -16,14 +16,16 @@
     axes,
     sizes,
     pieces,
-    group_ref,
-    entry_ref,
+    group_hbm,
+    entry_hbm,
     warmth_ref,
     offset_ref,
     picture_hbm,
     caption_hbm,
     grad_image_ref,
     grad_text_ref,
+    group_ref,
+    entry_ref,
     picture,
     caption,
     target,
@@ -50,12 +52,23 @@
     barrier = pltpu.get_barrier_semaphore()
     for neighbour in (left, right):
         pl.semaphore_signal(barrier, inc=1, device_id=neighbour, device_id_type=MESH)
-    load_picture = pltpu.make_async_copy(picture_hbm, picture, local_sem.at[0])
-    load_caption = pltpu.make_async_copy(caption_hbm, caption, local_sem.at[1])
-    load_picture.start()
-    load_caption.start()
+    loads = [
+        pltpu.make_async_copy(source, sink, local_sem.at[index])
+        for index, (source, sink) in enumerate(
+            (
+                (group_hbm, group_ref),
+                (entry_hbm, entry_ref),
+                (picture_hbm, picture),
+                (caption_hbm, caption),
+            )
+        )
+    ]
+    for load in loads:
+        load.start()
+    loads[0].wait()
+    loads[1].wait()
     target[...] = jnp.broadcast_to(
-        group_ref[...] * rows + entry_ref[...], target.shape
+        (group_ref[...] * rows + entry_ref[...]).reshape(1, rows), target.shape
     )
     pl.semaphore_wait(barrier, 2)
 
@@ -86,6 +99,8 @@
         started += 1
     sent = 0
 
+    for load in loads[2:]:
+        load.wait()
     warmth = warmth_ref[0]
     offset = offset_ref[0]
 
@@ -103,8 +118,6 @@
             values, text, (((0,), (0,)), ((), ())), preferred_element_type=jnp.float32
         )
 
-    load_picture.wait()
-    load_caption.wait()
     own = tile(caption[...], picture[...], target[0:1, :], rows)
     text_sum[...] = jnp.dot(own, picture[...], preferred_element_type=jnp.float32)
     image_sum[...] = over_text(own, caption[...])
@@ -148,6 +161,17 @@
                 copy.wait_send()
 
 
+def store(image_ref, text_ref, image_hbm, text_hbm, sem):
+    copies = [
+        pltpu.make_async_copy(image_ref, image_hbm, sem.at[0]),
+        pltpu.make_async_copy(text_ref, text_hbm, sem.at[1]),
+    ]
+    for copy in copies:
+        copy.start()
+    for copy in copies:
+        copy.wait()
+
+
 def per_device(
     axes,
     sizes,
@@ -165,14 +189,15 @@
     block = (rows, width)
     vmem = pl.BlockSpec(memory_space=pltpu.VMEM)
     smem = pl.BlockSpec(memory_space=pltpu.SMEM)
-    hbm = pl.BlockSpec(memory_space=pl.ANY)
-    out = jax.ShapeDtypeStruct(block, jnp.bfloat16)
-    return pl.pallas_call(
+    hbm = pl.BlockSpec(memory_space=pltpu.HBM)
+    grad_image, grad_text = pl.pallas_call(
         functools.partial(kernel, axes, sizes, pieces),
-        out_shape=(out, out),
-        in_specs=[vmem, vmem, smem, smem, hbm, hbm],
+        out_shape=(pltpu.VMEM(block, jnp.bfloat16), pltpu.VMEM(block, jnp.bfloat16)),
+        in_specs=[hbm, hbm, smem, smem, hbm, hbm],
         out_specs=(vmem, vmem),
         scratch_shapes=[
+            pltpu.VMEM((rows,), jnp.int32),
+            pltpu.VMEM((rows,), jnp.int32),
             pltpu.VMEM(block, jnp.bfloat16),
             pltpu.VMEM(block, jnp.bfloat16),
             pltpu.VMEM((8, rows), jnp.int32),
@@ -181,7 +206,7 @@
             pltpu.VMEM((2, 8, rows), jnp.int32),
             pltpu.VMEM(block, jnp.float32),
             pltpu.VMEM(block, jnp.float32),
-            pltpu.SemaphoreType.DMA((2,)),
+            pltpu.SemaphoreType.DMA((4,)),
             pltpu.SemaphoreType.DMA((2, len(pieces))),
             pltpu.SemaphoreType.DMA((2, len(pieces))),
         ],
@@ -189,12 +214,22 @@
             collective_id=0, has_side_effects=True, vmem_limit_bytes=32 << 20
         ),
     )(
-        matching_caption_group.reshape(1, rows),
-        matching_caption_entry.reshape(1, rows),
+        pltpu.with_memory_space_constraint(matching_caption_group, pltpu.HBM),
+        pltpu.with_memory_space_constraint(matching_caption_entry, pltpu.HBM),
         inverse_warmth.reshape(1),
         additive_offset.reshape(1),
-        picture_embedding,
-        caption_embedding,
+        pltpu.with_memory_space_constraint(picture_embedding, pltpu.HBM),
+        pltpu.with_memory_space_constraint(caption_embedding, pltpu.HBM),
+    )
+    return pl.pallas_call(
+        store,
+        out_shape=(pltpu.HBM(block, jnp.bfloat16), pltpu.HBM(block, jnp.bfloat16)),
+        in_specs=[vmem, vmem],
+        out_specs=(hbm, hbm),
+        scratch_shapes=[pltpu.SemaphoreType.DMA((2,))],
+    )(
+        pltpu.with_memory_space_constraint(grad_image, pltpu.VMEM),
+        pltpu.with_memory_space_constraint(grad_text, pltpu.VMEM),
     )
 
 

time: 90.3 us -> 86.7 us (0.960)
  local copies, waits for them, and re-layouts: 4.85 us -> 0 us
  Pallas kernels: 83.3 us -> 84.6 us
    unnamed x10 -> x0, local copies, waits for them, and re-layouts: 4.84 us -> none
    pallas_call x0 -> x1, Pallas kernels: none -> 1.22 us  [per_device(): pl.pallas_call(store, out_shape=(pltpu.HBM(block, jnp.bfloat16), pltpu.HB...]
where the time goes in v2:
time: 86.7 us; the launch traced here: 86.5 us
  Pallas kernels  84.6 us (98%)
  between operations  1.93 us (2%)
    pallas_call x1, Pallas kernels, per_device(): pl.pallas_call(functools.partial(kernel, axes, sizes, pieces), out_shape=...  83.4 us

profile of v2, /device:TPU:27, one launch (start us, length us, event | category | flops | bytes accessed | tf_op | source)
XLA Modules:
  0.0 86.5 jit_solution(11574377924967414553)
XLA Ops:
  1.9 83.4 %shard_map.77 = (bf16[384,1152]{1,0:T(8,128)(2,1)S(1)}, bf16[384,1152]{1,0:T(8,128)(2,1)S(1)}) custom-call(s32[384]{0:T(512)} %group_hbm.1, s32[384]{0:T(512)} %entry_hbm.1, f32[1]{0:T(128)} %bitcast.2.warmth_ref, f32[1]{0:T(128)} %bitcast.3.offset_ref, bf16[384,1152]{1,0:T(8,128)(2,1)} %picture_hbm.1, bf16[384,1152]{1,0:T(8,128)(2,1)} %caption_hbm.1), custom_call_target="tpu_custom_call" | custom-call | tf_op jit(solution)/shard_map/pallas_call | solution.py:193
  85.3 1.2 %shard_map.78 = (bf16[384,1152]{1,0:T(8,128)(2,1)}, bf16[384,1152]{1,0:T(8,128)(2,1)}) custom-call(bf16[384,1152]{1,0:T(8,128)(2,1)S(1)} %get-tuple-element.4.image_ref, bf16[384,1152]{1,0:T(8,128)(2,1)S(1)} %get-tuple-element.5.text_ref), custom_call_target="tpu_custom_call" | custom-call | tf_op jit(solution)/shard_map/pallas_call | solution.py:224
